TPU v7x, 128 devices: a whole 4x4x4 slice. The times are simulated.
128 devices in a mesh: morton: 128 (over y, z, x, core).
Axes of the slice: x: 4, y: 4, z: 4, core: 2. Of those that a mesh axis runs over, the one named last changes fastest.
Arguments:
- leaf_mult: bfloat16 [98304, 152], P('morton'), may hold values from -6 to 6
- leaf_list: int32 [98304, 316], P('morton'), may hold values from -6144 to 6144, as said below
- parent_list: int32 [12288, 316], P('morton'), may hold values from -1 to 12287, as said below
- top_list: int32 [1536, 316], P('morton'), may hold values from -1 to 1535, as said below
- m2m_ops: bfloat16 [8, 152, 152], replicated, may hold values from -0.15625 to 0.15625
- m2l_ops: bfloat16 [316, 152, 152], replicated, may hold values from -0.0390625 to 0.0390625
- l2l_ops: bfloat16 [8, 152, 152], replicated, may hold values from -0.5 to 0.5
Outputs:
- leaf_local: float32 [98304, 152], P('morton')
Inputs may be any that keep to these rules, and one draw needn't show every extreme that they name: `leaf_list`: 0 marks an empty slot; any other entry is an offset of at most 6144 in size to a leaf box inside the grid, every row has an entry of exactly that size, and both signs occur. `parent_list`: -1 marks an empty slot; any other entry is a parent-level box at most 768 positions from the row's box, and every row has an entry at exactly that distance. `top_list`: -1 marks an empty slot; other entries are any top-level box.
All inputs are finite; a program needn't handle non-finite values.
Results may differ from a plain program's by a relative error of at most 0.0035.
Values may be sent and summed in bfloat16 or wider, within the bound.
No kernel may reach another device: no remote copies, remote signals or barrier semaphores. Data moves between devices by JAX's collectives and lax.ppermute only.
A program may use at most 256 MiB of HBM per device.

v0:
```python
import math

import jax
import jax.numpy as jnp
from jax import lax
from jax.sharding import PartitionSpec as P

RD = 8


def passed_along(block, axis, distance):
    devices = range(lax.axis_size(axis))
    route = [(i - distance, i) for i in devices if i - distance in devices]
    return lax.ppermute(block, axis, route)


def ascend(children, m2m_ops):
    width = children.shape[1]
    grouped = children.reshape(children.shape[0] // 8, 8, width)
    summed = jnp.einsum("bcq,cqp->bp", grouped, m2m_ops, preferred_element_type=jnp.float32)
    return summed.astype(jnp.bfloat16)


def descend(coarse, l2l_ops):
    spread = jnp.einsum("tq,cqp->tcp", coarse, l2l_ops, preferred_element_type=jnp.float32)
    return spread.reshape(coarse.shape[0] * 8, coarse.shape[1])


def translate(lists, padded_table, base, m2l_ops):
    count, vectors = lists.shape
    block = math.gcd(512, count)

    def one_block(entries):
        slots = jnp.where(entries >= 0, entries - base + 1, 0)
        picked = jnp.take(padded_table, slots, axis=0, mode="clip")
        return lax.dot_general(
            picked, m2l_ops, (((1, 2), (0, 1)), ((), ())), preferred_element_type=jnp.float32
        )

    out = lax.map(one_block, lists.reshape(count // block, block, vectors))
    return out.reshape(count, padded_table.shape[1])


def with_blank(pieces):
    blank = jnp.zeros((1, pieces[0].shape[1]), pieces[0].dtype)
    return jnp.concatenate([blank] + pieces, axis=0)


def leaf_reach(leaf_mult):
    pieces = []
    for offset in range(-RD, RD + 1):
        if offset == 0:
            pieces.append(leaf_mult)
        else:
            pieces.append(passed_along(leaf_mult, "morton", -offset))
    return with_blank(pieces)


def parent_reach(parent_mult):
    pieces = []
    for offset in range(-RD, RD + 1):
        if offset == 0:
            pieces.append(parent_mult)
        else:
            pieces.append(passed_along(parent_mult, "morton", -offset))
    return with_blank(pieces)


def local(leaf_mult, leaf_list, parent_list, top_list, m2m_ops, m2l_ops, l2l_ops):
    boxes, width = leaf_mult.shape
    here = lax.axis_index("morton")
    parents = boxes // 8
    parent_mult = ascend(leaf_mult, m2m_ops)
    top_mult = ascend(parent_mult, m2m_ops)
    all_top = lax.all_gather(top_mult, "morton", axis=0, tiled=True)
    near_parent = parent_reach(parent_mult)
    parent_far = translate(parent_list, near_parent, here * parents - RD * parents, m2l_ops)
    top_local = (0.25 * translate(top_list, with_blank([all_top]), 0, m2l_ops)).astype(jnp.bfloat16)
    parent_local = (0.5 * parent_far + descend(top_local, l2l_ops)).astype(jnp.bfloat16)
    near_leaf = leaf_reach(leaf_mult)
    rows = jnp.arange(boxes, dtype=jnp.int32)[:, None]
    leaf_rows = jnp.where(leaf_list != 0, leaf_list + rows + RD * boxes, -1)
    leaf_far = translate(leaf_rows, near_leaf, 0, m2l_ops)
    return leaf_far + descend(parent_local, l2l_ops)


def solution(mesh):
    return jax.shard_map(
        local,
        mesh=mesh,
        in_specs=(
            P("morton", None),
            P("morton", None),
            P("morton", None),
            P("morton", None),
            P(),
            P(),
            P(),
        ),
        out_specs=P("morton", None),
        check_vma=False,
    )
```

profile of v0, /device:TPU:1, one launch (start us, length us, event | category | flops | bytes accessed | tf_op | source)
XLA Modules:
  0.0 1745.4 jit_solution(16175237982277672144)
XLA Ops:
  23.3 35.8 %all-gather = bf16[128,12,152]{2,1,0:T(8,128)(2,1)S(1)} all-gather(bf16[1,12,152]{2,1,0:T(8,128)(2,1)S(1)} %fusion.4), channel_id=1, replica_groups=mesh['morton'=128] {'morton'}, dimensions={0}, use_global_device_ids=true | all-gather | bytes 470592 | tf_op jit(solution)/shard_map/all_gather | solution.py:75
  62.6 42.3 %while.32 = (s32[]{:T(128)}, f32[3,4,152]{2,1,0:T(4,128)}, s32[3,4,316]{2,1,0:T(4,128)S(1)}, bf16[1537,152]{1,0:T(8,128)(2,1)S(1)}, bf16[316,152,152]{0,2,1:T(8,128)(2,1)}, /*index=5*/s32[]{:T(128)}) while((s32[]{:T(128)}, f32[3,4,152]{2,1,0:T(4,128)}, s32[3,4,316]{2,1,0:T(4,128)S(1)}, bf16[1537,152]{1,0:T(8,128)(2,1)S(1)}, ...), condition=%wide.region_5.6_spmd, body=%wide.region_4.5_spmd.sunk | while | flops 58412752 | bytes 20476872 | solution.py:40
  67.7 9.1 fusion.37
  81.8 9.1 fusion.37
  95.9 9.1 fusion.37
  121.3 9.5 collective-permute-start
  152.4 172.4 %while.31 = (s32[]{:T(128)}, f32[3,32,152]{2,1,0:T(8,128)}, s32[3,32,316]{2,1,0:T(8,128)}, s32[]{:T(128)}, bf16[1633,152]{1,0:T(8,128)(2,1)S(1)}, /*index=5*/bf16[316,152,152]{0,2,1:T(8,128)(2,1)}, s32[]{:T(128)}) while((s32[]{:T(128)}, f32[3,32,152]{2,1,0:T(8,128)}, s32[3,32,316]{2,1,0:T(8,128)}, s32[]{:T(128)}, ...), condition=%wide.region_3.4_spmd, body=%wide.region_2.3_spmd.sunk | while | flops 467305984 | bytes 40240724 | solution.py:40
  153.4 29.1 %gather_fusion.1 = bf16[10112,152]{1,0:T(8,128)(2,1)} fusion(bf16[1633,152]{1,0:T(8,128)(2,1)S(1)} %get-tuple-element.282, s32[10240]{0:T(1024)S(1)} %pad_clamp_fusion.4), kind=kCustom, calls=%fused_computation.1.clone.1 | custom fusion | bytes 6188544 | tf_op jit(solution)/shard_map/while/body/eval_jaxpr/jit(_take)/gather | solution.py:35
  188.8 10.5 reshape.189
  199.4 10.5 fusion.34
  210.9 29.1 %gather_fusion.1 = bf16[10112,152]{1,0:T(8,128)(2,1)} fusion(bf16[1633,152]{1,0:T(8,128)(2,1)S(1)} %get-tuple-element.282, s32[10240]{0:T(1024)S(1)} %pad_clamp_fusion.4), kind=kCustom, calls=%fused_computation.1.clone.1 | custom fusion | bytes 6188544 | tf_op jit(solution)/shard_map/while/body/eval_jaxpr/jit(_take)/gather | solution.py:35
  246.3 10.5 reshape.189
  256.8 10.5 fusion.34
  268.3 29.1 %gather_fusion.1 = bf16[10112,152]{1,0:T(8,128)(2,1)} fusion(bf16[1633,152]{1,0:T(8,128)(2,1)S(1)} %get-tuple-element.282, s32[10240]{0:T(1024)S(1)} %pad_clamp_fusion.4), kind=kCustom, calls=%fused_computation.1.clone.1 | custom fusion | bytes 6188544 | tf_op jit(solution)/shard_map/while/body/eval_jaxpr/jit(_take)/gather | solution.py:35
  303.7 10.5 reshape.189
  314.3 10.5 fusion.34
  327.4 10.1 collective-permute-start.2
  378.5 7.4 collective-permute-done.9
  385.9 54.5 %concatenate.9 = bf16[13057,152]{1,0:T(8,128)(2,1)} concatenate(bf16[1,152]{1,0:T(2,128)(2,1)S(1)} %broadcast.117.clone, bf16[768,152]{1,0:T(8,128)(2,1)} %collective-permute-done, bf16[768,152]{1,0:T(8,128)(2,1)S(1)} %collective-permute-done.1, bf16[768,152]{1,0:T(8,128)(2,1)} %copy-done.7, bf16[768,152]{1,0:T(8,128)(2,1)} %copy-done.8, bf16[768,152]{1,0:T(8,128)(2,1)} %copy-done.9, ...), dimensions={0} | concatenate | bytes 7938656 | tf_op jit(solution)/shard_map/concatenate | solution.py:46
  440.4 1303.0 %while.30 = (s32[]{:T(128)}, f32[3,256,152]{1,0,2:T(4,128)}, s32[3,256,316]{2,1,0:T(8,128)}, bf16[13057,152]{1,0:T(8,128)(2,1)}, bf16[316,152,152]{0,2,1:T(8,128)(2,1)}, /*index=5*/s32[]{:T(128)}, s32[]{:T(128)}) while((s32[]{:T(128)}, f32[3,256,152]{1,0,2:T(4,128)}, s32[3,256,316]{2,1,0:T(8,128)}, bf16[13057,152]{1,0:T(8,128)(2,1)}, ...), condition=%wide.region_1.2_spmd, body=%wide.region_0.1_spmd.sunk | while | flops 3738365952 | bytes 189791824 | solution.py:40
  441.9 302.1 %gather_fusion = bf16[80896,152]{1,0:T(8,128)(2,1)} fusion(bf16[13057,152]{1,0:T(8,128)(2,1)} %get-tuple-element.260, s32[80896]{0:T(1024)S(1)} %broadcast_clamp_fusion.2), kind=kCustom, calls=%fused_computation.clone.1 | custom fusion | bytes 49508352 | tf_op jit(solution)/shard_map/while/body/eval_jaxpr/jit(_take)/gather | solution.py:35
  744.0 50.3 %reshape.185 = bf16[256,316,152]{2,1,0:T(8,128)(2,1)} reshape(bf16[80896,152]{1,0:T(8,128)(2,1)} %gather_fusion) | data formatting | bytes 49184768 | tf_op jit(solution)/shard_map/while/body/eval_jaxpr/jit(_take)/gather | solution.py:35
  794.4 57.3 %copy.126 = bf16[256,316,152]{1,0,2:T(8,128)(2,1)} copy(bf16[256,316,152]{2,1,0:T(8,128)(2,1)} %reshape.185) | data formatting | bytes 49184768 | tf_op jit(solution)/shard_map/while/body/eval_jaxpr/jit(_take)/gather | solution.py:35
  851.7 18.2 %convolution_bitcast_fusion.6 = f32[1,256,152]{1,2,0:T(8,128)S(1)} fusion(bf16[256,316,152]{1,0,2:T(8,128)(2,1)} %copy.126, bf16[316,152,152]{0,2,1:T(8,128)(2,1)} %get-tuple-element.261), kind=kOutput, calls=%fused_computation.3.clone.1 | convolution fusion | flops 3738042368 | bytes 39349760 | tf_op jit(solution)/shard_map/while/body/eval_jaxpr/dot_general | solution.py:36
  876.2 302.1 %gather_fusion = bf16[80896,152]{1,0:T(8,128)(2,1)} fusion(bf16[13057,152]{1,0:T(8,128)(2,1)} %get-tuple-element.260, s32[80896]{0:T(1024)S(1)} %broadcast_clamp_fusion.2), kind=kCustom, calls=%fused_computation.clone.1 | custom fusion | bytes 49508352 | tf_op jit(solution)/shard_map/while/body/eval_jaxpr/jit(_take)/gather | solution.py:35
  1178.3 50.3 %reshape.185 = bf16[256,316,152]{2,1,0:T(8,128)(2,1)} reshape(bf16[80896,152]{1,0:T(8,128)(2,1)} %gather_fusion) | data formatting | bytes 49184768 | tf_op jit(solution)/shard_map/while/body/eval_jaxpr/jit(_take)/gather | solution.py:35
  1228.7 57.3 %copy.126 = bf16[256,316,152]{1,0,2:T(8,128)(2,1)} copy(bf16[256,316,152]{2,1,0:T(8,128)(2,1)} %reshape.185) | data formatting | bytes 49184768 | tf_op jit(solution)/shard_map/while/body/eval_jaxpr/jit(_take)/gather | solution.py:35
  1286.0 18.2 %convolution_bitcast_fusion.6 = f32[1,256,152]{1,2,0:T(8,128)S(1)} fusion(bf16[256,316,152]{1,0,2:T(8,128)(2,1)} %copy.126, bf16[316,152,152]{0,2,1:T(8,128)(2,1)} %get-tuple-element.261), kind=kOutput, calls=%fused_computation.3.clone.1 | convolution fusion | flops 3738042368 | bytes 39349760 | tf_op jit(solution)/shard_map/while/body/eval_jaxpr/dot_general | solution.py:36
  1310.5 302.1 %gather_fusion = bf16[80896,152]{1,0:T(8,128)(2,1)} fusion(bf16[13057,152]{1,0:T(8,128)(2,1)} %get-tuple-element.260, s32[80896]{0:T(1024)S(1)} %broadcast_clamp_fusion.2), kind=kCustom, calls=%fused_computation.clone.1 | custom fusion | bytes 49508352 | tf_op jit(solution)/shard_map/while/body/eval_jaxpr/jit(_take)/gather | solution.py:35
  1612.6 50.3 %reshape.185 = bf16[256,316,152]{2,1,0:T(8,128)(2,1)} reshape(bf16[80896,152]{1,0:T(8,128)(2,1)} %gather_fusion) | data formatting | bytes 49184768 | tf_op jit(solution)/shard_map/while/body/eval_jaxpr/jit(_take)/gather | solution.py:35
  1663.0 57.3 %copy.126 = bf16[256,316,152]{1,0,2:T(8,128)(2,1)} copy(bf16[256,316,152]{2,1,0:T(8,128)(2,1)} %reshape.185) | data formatting | bytes 49184768 | tf_op jit(solution)/shard_map/while/body/eval_jaxpr/jit(_take)/gather | solution.py:35
  1720.3 18.2 %convolution_bitcast_fusion.6 = f32[1,256,152]{1,2,0:T(8,128)S(1)} fusion(bf16[256,316,152]{1,0,2:T(8,128)(2,1)} %copy.126, bf16[316,152,152]{0,2,1:T(8,128)(2,1)} %get-tuple-element.261), kind=kOutput, calls=%fused_computation.3.clone.1 | convolution fusion | flops 3738042368 | bytes 39349760 | tf_op jit(solution)/shard_map/while/body/eval_jaxpr/dot_general | solution.py:36
  (169 shorter events, 165.4 us)
Async XLA Ops:
  1.6 103.3 %collective-permute-start.16 = (bf16[96,152]{0,1:T(8,128)(2,1)S(1)}, bf16[96,152]{0,1:T(8,128)(2,1)S(1)}, u32[]{:S(2)}, u32[]{:S(2)}) collective-permute-start(bf16[96,152]{0,1:T(8,128)(2,1)S(1)} %fusion.2), channel_id=1, source_target_pairs={{0,8},{1,9},{2,10},{3,11},{4,12},{5,13},{6,14},{7,15},{8,16},{9,17... | collective-permute-start | bytes 87560 | tf_op jit(solution)/shard_map/ppermute | solution.py:14
  6.0 102.1 %collective-permute-start.17 = (bf16[96,152]{0,1:T(8,128)(2,1)S(1)}, bf16[96,152]{0,1:T(8,128)(2,1)}, u32[]{:S(2)}, u32[]{:S(2)}) collective-permute-start(bf16[96,152]{0,1:T(8,128)(2,1)S(1)} %fusion.2), channel_id=1, source_target_pairs={{0,7},{1,8},{2,9},{3,10},{4,11},{5,12},{6,13},{7,14},{8,15},{9,16}... | collective-permute-start | bytes 87560 | tf_op jit(solution)/shard_map/ppermute | solution.py:14
  11.0 100.9 %collective-permute-start.18 = (bf16[96,152]{0,1:T(8,128)(2,1)S(1)}, bf16[96,152]{0,1:T(8,128)(2,1)}, u32[]{:S(2)}, u32[]{:S(2)}) collective-permute-start(bf16[96,152]{0,1:T(8,128)(2,1)S(1)} %fusion.2), channel_id=1, source_target_pairs={{0,6},{1,7},{2,8},{3,9},{4,10},{5,11},{6,12},{7,13},{8,14},{9,15},... | collective-permute-start | bytes 87560 | tf_op jit(solution)/shard_map/ppermute | solution.py:14
  15.4 99.3 %collective-permute-start.19 = (bf16[96,152]{0,1:T(8,128)(2,1)S(1)}, bf16[96,152]{0,1:T(8,128)(2,1)}, u32[]{:S(2)}, u32[]{:S(2)}) collective-permute-start(bf16[96,152]{0,1:T(8,128)(2,1)S(1)} %fusion.2), channel_id=1, source_target_pairs={{0,5},{1,6},{2,7},{3,8},{4,9},{5,10},{6,11},{7,12},{8,13},{9,14},{... | collective-permute-start | bytes 87560 | tf_op jit(solution)/shard_map/ppermute | solution.py:14
  18.6 98.0 %collective-permute-start.20 = (bf16[96,152]{0,1:T(8,128)(2,1)S(1)}, bf16[96,152]{0,1:T(8,128)(2,1)}, u32[]{:S(2)}, u32[]{:S(2)}) collective-permute-start(bf16[96,152]{0,1:T(8,128)(2,1)S(1)} %fusion.2), channel_id=1, source_target_pairs={{0,4},{1,5},{2,6},{3,7},{4,8},{5,9},{6,10},{7,11},{8,12},{9,13},{1... | collective-permute-start | bytes 87560 | tf_op jit(solution)/shard_map/ppermute | solution.py:14
  104.9 13.0 collective-permute-start.21
  108.1 11.2 collective-permute-start.22
  111.9 9.3 collective-permute-start.23
  114.7 16.1 collective-permute-start.24
  116.6 15.5 collective-permute-start.25
  117.9 15.5 collective-permute-start.26
  119.2 15.5 collective-permute-start.27
  121.3 29.7 %collective-permute-start = (bf16[768,152]{1,0:T(8,128)(2,1)S(1)}, bf16[768,152]{1,0:T(8,128)(2,1)}, u32[]{:S(2)}, u32[]{:S(2)}) collective-permute-start(bf16[768,152]{1,0:T(8,128)(2,1)S(1)} %copy.77), channel_id=1, source_target_pairs={{0,8},{1,9},{2,10},{3,11},{4,12},{5,13},{6,14},{7,15},{8,16},{9,17... | collective-permute-start | bytes 700424 | tf_op jit(solution)/shard_map/ppermute | solution.py:14
  130.8 7.2 collective-permute-start.28
  132.1 12.6 collective-permute-start.29
  133.4 12.6 collective-permute-start.30
  134.8 12.6 collective-permute-start.31
  138.0 186.8 %collective-permute-start.1 = (bf16[768,152]{1,0:T(8,128)(2,1)S(1)}, bf16[768,152]{1,0:T(8,128)(2,1)S(1)}, u32[]{:S(2)}, u32[]{:S(2)}) collective-permute-start(bf16[768,152]{1,0:T(8,128)(2,1)S(1)} %copy.77), channel_id=1, source_target_pairs={{0,7},{1,8},{2,9},{3,10},{4,11},{5,12},{6,13},{7,14},{8,15},{9,16}... | collective-permute-start | bytes 700424 | tf_op jit(solution)/shard_map/ppermute | solution.py:14
  144.8 181.4 %collective-permute-start.10 = (bf16[768,152]{1,0:T(8,128)(2,1)S(1)}, bf16[768,152]{1,0:T(8,128)(2,1)}, u32[]{:S(2)}, u32[]{:S(2)}) collective-permute-start(bf16[768,152]{1,0:T(8,128)(2,1)S(1)} %copy.77), channel_id=1, source_target_pairs={{3,0},{4,1},{5,2},{6,3},{7,4},{8,5},{9,6},{10,7},{11,8},{12,9},{13... | collective-permute-start | bytes 700424 | tf_op jit(solution)/shard_map/ppermute | solution.py:14
  146.1 181.4 %collective-permute-start.11 = (bf16[768,152]{1,0:T(8,128)(2,1)S(1)}, bf16[768,152]{1,0:T(8,128)(2,1)}, u32[]{:S(2)}, u32[]{:S(2)}) collective-permute-start(bf16[768,152]{1,0:T(8,128)(2,1)S(1)} %copy.77), channel_id=1, source_target_pairs={{4,0},{5,1},{6,2},{7,3},{8,4},{9,5},{10,6},{11,7},{12,8},{13,9},{1... | collective-permute-start | bytes 700424 | tf_op jit(solution)/shard_map/ppermute | solution.py:14
  147.4 190.1 %collective-permute-start.12 = (bf16[768,152]{1,0:T(8,128)(2,1)S(1)}, bf16[768,152]{1,0:T(8,128)(2,1)}, u32[]{:S(2)}, u32[]{:S(2)}) collective-permute-start(bf16[768,152]{1,0:T(8,128)(2,1)S(1)} %copy.77), channel_id=1, source_target_pairs={{5,0},{6,1},{7,2},{8,3},{9,4},{10,5},{11,6},{12,7},{13,8},{14,9},{... | collective-permute-start | bytes 700424 | tf_op jit(solution)/shard_map/ppermute | solution.py:14
  151.0 192.4 %collective-permute-start.13 = (bf16[768,152]{1,0:T(8,128)(2,1)S(1)}, bf16[768,152]{1,0:T(8,128)(2,1)S(1)}, u32[]{:S(2)}, u32[]{:S(2)}) collective-permute-start(bf16[768,152]{1,0:T(8,128)(2,1)S(1)} %copy.77), channel_id=1, source_target_pairs={{6,0},{7,1},{8,2},{9,3},{10,4},{11,5},{12,6},{13,7},{14,8},{15,9},... | collective-permute-start | bytes 700424 | tf_op jit(solution)/shard_map/ppermute | solution.py:14
  324.8 24.4 %collective-permute-start.14 = (bf16[768,152]{1,0:T(8,128)(2,1)S(1)}, bf16[768,152]{1,0:T(8,128)(2,1)S(1)}, u32[]{:S(2)}, u32[]{:S(2)}) collective-permute-start(bf16[768,152]{1,0:T(8,128)(2,1)S(1)} %copy.77), channel_id=1, source_target_pairs={{7,0},{8,1},{9,2},{10,3},{11,4},{12,5},{13,6},{14,7},{15,8},{16,9}... | collective-permute-start | bytes 700424 | tf_op jit(solution)/shard_map/ppermute | solution.py:14
  326.1 29.0 %collective-permute-start.15 = (bf16[768,152]{1,0:T(8,128)(2,1)S(1)}, bf16[768,152]{1,0:T(8,128)(2,1)S(1)}, u32[]{:S(2)}, u32[]{:S(2)}) collective-permute-start(bf16[768,152]{1,0:T(8,128)(2,1)S(1)} %copy.77), channel_id=1, source_target_pairs={{8,0},{9,1},{10,2},{11,3},{12,4},{13,5},{14,6},{15,7},{16,8},{17,9... | collective-permute-start | bytes 700424 | tf_op jit(solution)/shard_map/ppermute | solution.py:14
  327.4 30.5 %collective-permute-start.2 = (bf16[768,152]{1,0:T(8,128)(2,1)S(1)}, bf16[768,152]{1,0:T(8,128)(2,1)S(1)}, u32[]{:S(2)}, u32[]{:S(2)}) collective-permute-start(bf16[768,152]{1,0:T(8,128)(2,1)S(1)} %copy.77), channel_id=1, source_target_pairs={{0,6},{1,7},{2,8},{3,9},{4,10},{5,11},{6,12},{7,13},{8,14},{9,15},... | collective-permute-start | bytes 700424 | tf_op jit(solution)/shard_map/ppermute | solution.py:14
  337.6 22.4 %collective-permute-start.3 = (bf16[768,152]{1,0:T(8,128)(2,1)S(1)}, bf16[768,152]{1,0:T(8,128)(2,1)S(1)}, u32[]{:S(2)}, u32[]{:S(2)}) collective-permute-start(bf16[768,152]{1,0:T(8,128)(2,1)S(1)} %copy.77), channel_id=1, source_target_pairs={{0,5},{1,6},{2,7},{3,8},{4,9},{5,10},{6,11},{7,12},{8,13},{9,14},{... | collective-permute-start | bytes 700424 | tf_op jit(solution)/shard_map/ppermute | solution.py:14
  343.4 19.7 %collective-permute-start.4 = (bf16[768,152]{1,0:T(8,128)(2,1)S(1)}, bf16[768,152]{1,0:T(8,128)(2,1)S(1)}, u32[]{:S(2)}, u32[]{:S(2)}) collective-permute-start(bf16[768,152]{1,0:T(8,128)(2,1)S(1)} %copy.77), channel_id=1, source_target_pairs={{0,4},{1,5},{2,6},{3,7},{4,8},{5,9},{6,10},{7,11},{8,12},{9,13},{1... | collective-permute-start | bytes 700424 | tf_op jit(solution)/shard_map/ppermute | solution.py:14
  349.2 17.0 collective-permute-start.5
  355.1 18.1 %collective-permute-start.6 = (bf16[768,152]{1,0:T(8,128)(2,1)S(1)}, bf16[768,152]{1,0:T(8,128)(2,1)}, u32[]{:S(2)}, u32[]{:S(2)}) collective-permute-start(bf16[768,152]{1,0:T(8,128)(2,1)S(1)} %copy.77), channel_id=1, source_target_pairs={{0,2},{1,3},{2,4},{3,5},{4,6},{5,7},{6,8},{7,9},{8,10},{9,11},{10,... | collective-permute-start | bytes 700424 | tf_op jit(solution)/shard_map/ppermute | solution.py:14
  358.0 20.5 %collective-permute-start.7 = (bf16[768,152]{1,0:T(8,128)(2,1)S(1)}, bf16[768,152]{1,0:T(8,128)(2,1)}, u32[]{:S(2)}, u32[]{:S(2)}) collective-permute-start(bf16[768,152]{1,0:T(8,128)(2,1)S(1)} %copy.77), channel_id=1, source_target_pairs={{0,1},{1,2},{2,3},{3,4},{4,5},{5,6},{6,7},{7,8},{8,9},{9,10},{10,1... | collective-permute-start | bytes 700424 | tf_op jit(solution)/shard_map/ppermute | solution.py:14
  360.0 18.5 %collective-permute-start.8 = (bf16[768,152]{1,0:T(8,128)(2,1)S(1)}, bf16[768,152]{1,0:T(8,128)(2,1)}, u32[]{:S(2)}, u32[]{:S(2)}) collective-permute-start(bf16[768,152]{1,0:T(8,128)(2,1)S(1)} %copy.77), channel_id=1, source_target_pairs={{1,0},{2,1},{3,2},{4,3},{5,4},{6,5},{7,6},{8,7},{9,8},{10,9},{11,1... | collective-permute-start | bytes 700424 | tf_op jit(solution)/shard_map/ppermute | solution.py:14
  363.1 22.8 %collective-permute-start.9 = (bf16[768,152]{1,0:T(8,128)(2,1)S(1)}, bf16[768,152]{1,0:T(8,128)(2,1)}, u32[]{:S(2)}, u32[]{:S(2)}) collective-permute-start(bf16[768,152]{1,0:T(8,128)(2,1)S(1)} %copy.77), channel_id=1, source_target_pairs={{2,0},{3,1},{4,2},{5,3},{6,4},{7,5},{8,6},{9,7},{10,8},{11,9},{12,... | collective-permute-start | bytes 700424 | tf_op jit(solution)/shard_map/ppermute | solution.py:14
  (18 other events, 1520.0 us)
where the time goes:
time: 1770 us; the launch traced here: 1750 us
  local copies, waits for them, and re-layouts  1460 us (82%)
  matrix products  114 us (6%)
  starting transfers between devices  101 us (6%)
  blocking collectives  35.8 us (2%)
  waiting for transfers between devices  19.8 us (1%)
    gather x27, local copies, waits for them, and re-layouts, one_block(): picked = jnp.take(padded_table, slots, axis=0, mode='clip')  1380 us
    dot_general x9, matrix products, one_block(): lax.dot_general(picked, m2l_ops, (((1, 2), (0, 1)), ((), ())), preferred_...  113 us
    ppermute x32, starting transfers between devices, passed_along(): return lax.ppermute(block, axis, route)  101 us
    concatenate x3, local copies, waits for them, and re-layouts, with_blank(): return jnp.concatenate([blank] + pieces, axis=0)  57.6 us
    all_gather x1, blocking collectives, local(): all_top = lax.all_gather(top_mult, 'morton', axis=0, tiled=True)  35.8 us
  transfers between devices with their start and end apart: 32, of which 3 were waited for; matrix products, arithmetic and copies ran while one was open for 13% of the time, Pallas kernels for 0%

commit v1 on v0

v1 whole, which is shorter than its diff:
```python
import jax
import jax.numpy as jnp
from jax import lax
from jax.experimental import pallas as pl
from jax.experimental.pallas import tpu as pltpu
from jax.sharding import PartitionSpec as P

RD = 8
PAD = 8


def shifted(block, axis, distance):
    devices = range(lax.axis_size(axis))
    route = [(i - distance, i) for i in devices if i - distance in devices]
    return lax.ppermute(block, axis, route)


def ascend(children, m2m_ops):
    width = children.shape[1]
    grouped = children.reshape(children.shape[0] // 8, 8 * width)
    summed = jnp.dot(grouped, m2m_ops.reshape(8 * width, width), preferred_element_type=jnp.float32)
    return summed.astype(jnp.bfloat16)


def descend(coarse, l2l_ops):
    spread = jnp.einsum("tq,cqp->tcp", coarse, l2l_ops, preferred_element_type=jnp.float32)
    return spread.reshape(coarse.shape[0] * 8, coarse.shape[1])


def far_kernel(slots, near, top, w_ref, out_ref, table, rows_a, rows_b, stage, slots_a, slots_b, sem, stage_sem):
    step = pl.program_id(0)
    steps = pl.num_programs(0)
    count, width = out_ref.shape
    chunk = stage.shape[1]
    top_chunk = top.shape[1]

    def slot_copy(pair, which, buffer):
        return pltpu.make_async_copy(slots.at[pair], buffer, sem.at[which])

    def fill(buffer, base, rows):
        def group(j, carry):
            x = buffer[pl.ds(pl.multiple_of(16 * j, 16), 16), :].astype(jnp.float32)
            tail = jnp.concatenate([x[:, 128:], jnp.zeros((16, 256 - width), jnp.float32)], axis=1)
            start = 2 * (base + 16 * j)
            table[pl.ds(start, 16, stride=2), :] = x[:, :128]
            table[pl.ds(start + 1, 16, stride=2), :] = tail
            return carry

        lax.fori_loop(0, rows // 16, group, 0, unroll=2)

    @pl.when(step == 0)
    def _():
        slot_copy(0, 0, slots_a).start()
        slot_copy(1, 1, slots_b).start()
        pieces = near.shape[0]

        def near_copy(piece, half):
            return pltpu.make_async_copy(near.at[piece], stage.at[half], stage_sem.at[half])

        near_copy(0, 0).start()
        out_ref[...] = jnp.zeros_like(out_ref)
        rows_a[...] = jnp.zeros_like(rows_a)
        rows_b[...] = jnp.zeros_like(rows_b)
        table[pl.ds(0, 2 * PAD), :] = jnp.zeros((2 * PAD, 128), jnp.float32)

        def piece_step(piece, carry):
            half = lax.rem(piece, 2)

            @pl.when(piece + 1 < pieces)
            def _():
                near_copy(piece + 1, 1 - half).start()

            near_copy(piece, half).wait()
            fill(stage.at[half], PAD + piece * chunk, chunk)
            return carry

        lax.fori_loop(0, pieces, piece_step, 0)
        base = PAD + pieces * chunk
        for part in range(top.shape[0]):
            copy = pltpu.make_async_copy(top.at[part], stage.at[0, pl.ds(0, top_chunk)], stage_sem.at[0])
            copy.start()
            copy.wait()
            fill(stage.at[0], base + part * top_chunk, top_chunk)

    def pick(into, buffer, which):
        for r in range(count):
            into[pl.ds(2 * r, 2), :] = table[pl.ds(buffer[which, r], 2), :]

    def apply(picked, which):
        head = picked[pl.ds(0, count, stride=2), :].astype(jnp.bfloat16)
        tail = picked[pl.ds(1, count, stride=2), :].astype(jnp.bfloat16)
        op = jnp.concatenate([w_ref[which], jnp.zeros((256 - width, width), jnp.bfloat16)], axis=0)
        both = jnp.concatenate([head, tail], axis=1)
        out_ref[...] += jnp.dot(both, op, preferred_element_type=jnp.float32)

    slot_copy(0, 0, slots_a).wait()
    pick(rows_a, slots_a, 0)
    apply(rows_a, 0)
    pick(rows_b, slots_a, 1)
    apply(rows_b, 1)
    slot_copy(jnp.minimum(2 * step + 2, 2 * steps - 2), 0, slots_a).start()
    slot_copy(0, 1, slots_b).wait()
    pick(rows_a, slots_b, 0)
    apply(rows_a, 2)
    pick(rows_b, slots_b, 1)
    apply(rows_b, 3)
    slot_copy(jnp.minimum(2 * step + 3, 2 * steps - 1), 1, slots_b).start()

    @pl.when(step == steps - 1)
    def _():
        slot_copy(0, 0, slots_a).wait()
        slot_copy(0, 1, slots_b).wait()


def far_field(slots, near, top, m2l_ops):
    vectors, count = slots.shape
    pieces, chunk, width = near.shape
    table_rows = PAD + pieces * chunk + top.shape[0] * top.shape[1]
    return pl.pallas_call(
        far_kernel,
        grid=(vectors // 4,),
        in_specs=[
            pl.BlockSpec(memory_space=pl.ANY),
            pl.BlockSpec(memory_space=pl.ANY),
            pl.BlockSpec(memory_space=pl.ANY),
            pl.BlockSpec((4, width, width), lambda s: (s, 0, 0)),
        ],
        out_specs=pl.BlockSpec((count, width), lambda s: (0, 0)),
        out_shape=jax.ShapeDtypeStruct((count, width), jnp.float32),
        scratch_shapes=[
            pltpu.VMEM((2 * table_rows, 128), jnp.float32),
            pltpu.VMEM((2 * count, 128), jnp.float32),
            pltpu.VMEM((2 * count, 128), jnp.float32),
            pltpu.VMEM((2, chunk, width), jnp.bfloat16),
            pltpu.SMEM((2, count), jnp.int32),
            pltpu.SMEM((2, count), jnp.int32),
            pltpu.SemaphoreType.DMA((2,)),
            pltpu.SemaphoreType.DMA((2,)),
        ],
        compiler_params=pltpu.CompilerParams(vmem_limit_bytes=56 * 2**20),
        name="far_field",
    )(slots.reshape(vectors // 2, 2, count), near, top, m2l_ops)


def local(leaf_mult, leaf_list, parent_list, top_list, m2m_ops, m2l_ops, l2l_ops):
    boxes, width = leaf_mult.shape
    vectors = leaf_list.shape[1]
    here = lax.axis_index("morton")
    devices = lax.axis_size("morton")
    parents, tops = boxes // 8, boxes // 64
    chunk = boxes + parents
    parent_mult = ascend(leaf_mult, m2m_ops)
    piece = jnp.concatenate([leaf_mult, parent_mult], axis=0)
    three = jnp.stack([shifted(piece, "morton", RD), piece, shifted(piece, "morton", -RD)])
    groups = [list(range(g, g + RD)) for g in range(0, devices, RD)]
    near = lax.all_gather(three, "morton", axis=0, tiled=True, axis_index_groups=groups)
    top_mult = ascend(parent_mult, m2m_ops)
    all_top = lax.all_gather(top_mult, "morton", axis=0, tiled=True)

    def place(box, per_device):
        device = box // per_device
        return ((device % RD) * 3 + device // RD - here // RD + 1) * chunk + box % per_device

    leaf_row = here * boxes + jnp.arange(boxes, dtype=jnp.int32)[None, :]
    leaf_offset = leaf_list.T
    leaf_slot = jnp.where(leaf_offset != 0, PAD + place(leaf_row + leaf_offset, boxes), 0)
    parent_box = parent_list.T
    parent_slot = jnp.where(parent_box >= 0, PAD + boxes + place(parent_box, parents), 0)
    top_box = top_list.T
    top_slot = jnp.where(top_box >= 0, PAD + 3 * RD * chunk + top_box, 0)
    spare = -(boxes + parents + tops) % 16
    slots = 2 * jnp.concatenate([leaf_slot, parent_slot, top_slot, jnp.zeros((vectors, spare), jnp.int32)], axis=1)
    far = far_field(slots, near, all_top.reshape(2, -1, width), m2l_ops)
    leaf_far = far[:boxes]
    parent_far = far[boxes:chunk]
    top_far = far[chunk : chunk + tops]
    top_local = (0.25 * top_far).astype(jnp.bfloat16)
    parent_local = (0.5 * parent_far + descend(top_local, l2l_ops)).astype(jnp.bfloat16)
    return leaf_far + descend(parent_local, l2l_ops)


def solution(mesh):
    return jax.shard_map(
        local,
        mesh=mesh,
        in_specs=(
            P("morton", None),
            P("morton", None),
            P("morton", None),
            P("morton", None),
            P(),
            P(),
            P(),
        ),
        out_specs=P("morton", None),
        check_vma=False,
    )
```

time: 1770 us -> 381 us (0.22); the launches traced: 1750 us -> 379 us
  local copies, waits for them, and re-layouts: 1460 us -> 54.9 us
  Pallas kernels: 0 us -> 247 us
  matrix products: 114 us -> 2.78 us
  starting transfers between devices: 101 us -> 5.68 us
    gather x27 -> x0, local copies, waits for them, and re-layouts: 1380 us -> none  [one_block(): picked = jnp.take(padded_table, slots, axis=0, mode='clip')]
    pallas_call x0 -> x1, Pallas kernels: none -> 247 us  [far_field(): pl.pallas_call(far_kernel, grid=(vectors // 4,), in_specs=[pl.BlockSpec(m...]
    dot_general x11 -> x2, matrix products: 114 us -> 0.54 us  [ascend(): jnp.dot(grouped, m2m_ops.reshape(8 * width, width), preferred_element_typ...]
    ppermute x32 -> x2, starting transfers between devices: 101 us -> 5.68 us  [shifted(): return lax.ppermute(block, axis, route)]
    concatenate x3 -> x4, local copies, waits for them, and re-layouts: 57.6 us -> 0.83 us  [local(): jnp.concatenate([leaf_slot, parent_slot, top_slot, jnp.zeros((vectors, sp...]
    unnamed x40 -> x17, local copies, waits for them, and re-layouts: 4.13 us -> 39 us
  transfers between devices with their start and end apart: 32 -> 3, of which waited for: 3 -> 2; matrix products, arithmetic and copies ran while one was open for 13% -> 12% of each run, Pallas kernels for 0% -> 0%
where the time goes in v1:
time: 381 us; the launch traced here: 379 us
  Pallas kernels  247 us (65%)
  local copies, waits for them, and re-layouts  54.9 us (14%)
  blocking collectives  40.2 us (11%)
  between operations  13.6 us (4%)
  waiting for transfers between devices  8.05 us (2%)
  other arithmetic  6.47 us (2%)
  starting transfers between devices  5.68 us (1%)
    pallas_call x1, Pallas kernels, far_field(): pl.pallas_call(far_kernel, grid=(vectors // 4,), in_specs=[pl.BlockSpec(m...  247 us
    all_gather x1, blocking collectives, local(): all_top = lax.all_gather(top_mult, 'morton', axis=0, tiled=True)  40.2 us
    unnamed x17, local copies, waits for them, and re-layouts  39 us
    all_gather x1, local copies, waits for them, and re-layouts, local(): lax.all_gather(three, 'morton', axis=0, tiled=True, axis_index_groups=gro...  11.6 us
    ppermute x2, waiting for transfers between devices, shifted(): return lax.ppermute(block, axis, route)  8.03 us
  transfers between devices with their start and end apart: 3, of which 2 were waited for; matrix products, arithmetic and copies ran while one was open for 12% of the time, Pallas kernels for 0%

profile of v1, /device:TPU:1, one launch (start us, length us, event | category | flops | bytes accessed | tf_op | source)
XLA Modules:
  0.0 378.8 jit_solution(7585639035138259441)
XLA Ops:
  6.5 1.2 copy.31
  7.7 0.4 reshape.29
  8.1 0.4 convolution_convert_fusion
  8.5 4.4 %collective-permute-start = (bf16[864,152]{0,1:T(8,128)(2,1)S(1)}, bf16[864,152]{0,1:T(8,128)(2,1)S(1)}, u32[]{:S(2)}, u32[]{:S(2)}) collective-permute-start(bf16[864,152]{0,1:T(8,128)(2,1)S(1)} %get-tuple-element.6), channel_id=1, source_target_pairs={{0,8},{1,9},{2,10},{3,11},{4,12},{5,13},{6,14},{7,15},{8,16},{9,17... | collective-permute-start | bytes 787976 | tf_op jit(solution)/shard_map/ppermute | solution.py:15
  12.9 1.3 collective-permute-start.1
  14.2 3.9 %collective-permute-done = bf16[864,152]{0,1:T(8,128)(2,1)S(1)} collective-permute-done((bf16[864,152]{0,1:T(8,128)(2,1)S(1)}, bf16[864,152]{0,1:T(8,128)(2,1)S(1)}, u32[]{:S(2)}, u32[]{:S(2)}) %collective-permute-start) | collective-permute-done | bytes 262688 | tf_op jit(solution)/shard_map/ppermute | solution.py:15
  18.1 4.2 %collective-permute-done.1 = bf16[864,152]{0,1:T(8,128)(2,1)S(1)} collective-permute-done((bf16[864,152]{0,1:T(8,128)(2,1)S(1)}, bf16[864,152]{0,1:T(8,128)(2,1)S(1)}, u32[]{:S(2)}, u32[]{:S(2)}) %collective-permute-start.1) | collective-permute-done | bytes 262688 | tf_op jit(solution)/shard_map/ppermute | solution.py:15
  22.3 1.1 pad_maximum_fusion
  23.4 0.1 copy.32
  23.5 3.3 fusion.8
  26.8 0.6 concatenate.13
  27.4 0.3 copy-done.5
  27.7 0.3 fusion.23
  28.0 0.1 copy.29
  28.2 0.1 concatenate.14
  28.3 0.1 copy.30
  28.4 0.1 concatenate.15
  28.5 0.1 pad.8.clone
  28.6 0.1 reshape.31
  28.7 0.2 fusion
  28.9 40.2 %all-gather = bf16[128,12,152]{2,1,0:T(8,128)(2,1)S(1)} all-gather(bf16[1,12,152]{2,1,0:T(8,128)(2,1)S(1)} %fusion), channel_id=1, replica_groups=mesh['morton'=128] {'morton'}, dimensions={0}, use_global_device_ids=true | all-gather | bytes 470592 | tf_op jit(solution)/shard_map/all_gather | solution.py:158
  69.1 1.3 reshape.32.top
  70.4 37.1 %copy.34.w_ref = bf16[316,152,152]{2,1,0:T(8,128)(2,1)} copy(bf16[316,152,152]{0,2,1:T(8,128)(2,1)} %param.12) | data formatting | bytes 29203456 | tf_op args[5]
  107.6 0.3 copy.37
  107.9 1.6 add_multiply_fusion.slots
  109.5 11.6 %copy.33.near = bf16[24,864,152]{2,1,0:T(8,128)(2,1)} copy(bf16[24,864,152]{1,2,0:T(8,128)(2,1)} %all-gather.3.cloned.1.call-done) | data formatting | bytes 12607488 | tf_op jit(solution)/shard_map/all_gather | solution.py:156
  121.1 247.0 %far_field.1 = f32[880,152]{1,0:T(8,128)} custom-call(s32[158,2,880]{2,1,0:T(2,128)} %add_multiply_fusion.slots, bf16[24,864,152]{2,1,0:T(8,128)(2,1)} %copy.33.near, bf16[2,768,152]{2,1,0:T(8,128)(2,1)} %reshape.32.top, bf16[316,152,152]{2,1,0:T(8,128)(2,1)} %copy.34.w_ref), custom_call_target="tpu_custom_call" | custom-call | tf_op jit(solution)/shard_map/far_field/pallas_call | solution.py:119
  368.1 0.9 fusion.38
  369.0 1.3 fusion.33
  370.3 0.4 copy.38
  370.8 0.1 slice_add_fusion
  370.9 1.0 copy.39
  (20 shorter events, 0.1 us)
Async XLA Ops:
  6.5 1.6 copy-start
  6.5 1.9 copy-start.4
  6.5 103.0 %all-gather.3.cloned.1.call-start = ((), (), s32[]{:S(2)}) async-start(), calls=%async_computation | async-start | bytes 7354368 | tf_op jit(solution)/shard_map/all_gather | solution.py:156
  8.5 9.6 %collective-permute-start = (bf16[864,152]{0,1:T(8,128)(2,1)S(1)}, bf16[864,152]{0,1:T(8,128)(2,1)S(1)}, u32[]{:S(2)}, u32[]{:S(2)}) collective-permute-start(bf16[864,152]{0,1:T(8,128)(2,1)S(1)} %get-tuple-element.6), channel_id=1, source_target_pairs={{0,8},{1,9},{2,10},{3,11},{4,12},{5,13},{6,14},{7,15},{8,16},{9,17... | collective-permute-start | bytes 787976 | tf_op jit(solution)/shard_map/ppermute | solution.py:15
  12.9 9.3 %collective-permute-start.1 = (bf16[864,152]{0,1:T(8,128)(2,1)S(1)}, bf16[864,152]{0,1:T(8,128)(2,1)S(1)}, u32[]{:S(2)}, u32[]{:S(2)}) collective-permute-start(bf16[864,152]{0,1:T(8,128)(2,1)S(1)} %get-tuple-element.6), channel_id=1, source_target_pairs={{8,0},{9,1},{10,2},{11,3},{12,4},{13,5},{14,6},{15,7},{16,8},{17,9... | collective-permute-start | bytes 787976 | tf_op jit(solution)/shard_map/ppermute | solution.py:15
  26.8 0.9 copy-start.5
  26.8 1.4 copy-start.6
  70.4 37.1 %copy-start.3 = (bf16[8,152,152]{2,1,0:T(8,128)(2,1)S(1)}, bf16[8,152,152]{2,1,0:T(8,128)(2,1)}, u32[]{:S(2)}) copy-start(bf16[8,152,152]{2,1,0:T(8,128)(2,1)} %param.13) | copy-start | bytes 1108996
  369.0 1.8 copy-start.2
  370.8 1.1 copy-start.1
Sparse Core Ops, SparseCore 0:
  23.5 46.5 all-gather.2

commit v2 on v1

v2 whole, which is shorter than its diff:
```python
import jax
import jax.numpy as jnp
from jax import lax
from jax.experimental import pallas as pl
from jax.experimental.pallas import tpu as pltpu
from jax.sharding import PartitionSpec as P

RD = 8
PAD = 8
GROUP = 4
TOP_ROWS = 16


def shifted(block, axis, distance):
    devices = range(lax.axis_size(axis))
    route = [(i - distance, i) for i in devices if i - distance in devices]
    return lax.ppermute(block, axis, route)


def ascend(children, m2m_ops):
    width = children.shape[1]
    grouped = children.reshape(children.shape[0] // 8, 8 * width)
    summed = jnp.dot(grouped, m2m_ops.reshape(8 * width, width), preferred_element_type=jnp.float32)
    return summed.astype(jnp.bfloat16)


def descend(coarse, l2l_ops):
    spread = jnp.einsum("tq,cqp->tcp", coarse, l2l_ops, preferred_element_type=jnp.float32)
    return spread.reshape(coarse.shape[0] * 8, coarse.shape[1])


def far_kernel(slots, near, top, w_before, w_now, out_ref, table, rows_a, rows_b, stage, top_stage, slots_a, slots_b, sem, stage_sem):
    step = pl.program_id(0)
    steps = pl.num_programs(0)
    groups = slots.shape[0]
    count, width = out_ref.shape

    def slot_copy(group, which, buffer):
        return pltpu.make_async_copy(slots.at[group], buffer, sem.at[which])

    def fill(buffer, base):
        rows, wide = buffer.shape

        def sixteen(j, carry):
            x = buffer[pl.ds(pl.multiple_of(16 * j, 16), 16), :].astype(jnp.float32)
            tail = x[:, 128:]
            if wide < 256:
                tail = jnp.concatenate([tail, jnp.zeros((16, 256 - wide), jnp.float32)], axis=1)
            start = 2 * (base + 16 * j)
            table[pl.ds(start, 16, stride=2), :] = x[:, :128]
            table[pl.ds(start + 1, 16, stride=2), :] = tail
            return carry

        lax.fori_loop(0, rows // 16, sixteen, 0, unroll=2)

    def fill_all(pieces, source, buffers, base):
        def copy(piece, half):
            return pltpu.make_async_copy(source.at[piece], buffers.at[half], stage_sem.at[half])

        copy(0, 0).start()

        def one(piece, carry):
            half = lax.rem(piece, 2)

            @pl.when(piece + 1 < pieces)
            def _():
                copy(piece + 1, 1 - half).start()

            copy(piece, half).wait()
            fill(buffers.at[half], base + piece * buffers.shape[1])
            return carry

        lax.fori_loop(0, pieces, one, 0)

    @pl.when(step == 0)
    def _():
        slot_copy(0, 0, slots_a).start()
        slot_copy(1, 1, slots_b).start()
        out_ref[...] = jnp.zeros_like(out_ref)
        rows_b[...] = jnp.zeros_like(rows_b)
        table[pl.ds(0, 2 * PAD), :] = jnp.zeros((2 * PAD, 128), jnp.float32)
        fill_all(near.shape[0], near, stage, PAD)
        fill_all(top.shape[0], top, top_stage, PAD + near.shape[0] * near.shape[1])

    def pick(into, buffer):
        for g in range(GROUP):
            for r in range(count):
                into[g, pl.ds(2 * r, 2), :] = table[pl.ds(buffer[g, r], 2), :]

    def apply(picked, w_ref):
        parts, ops = [], []
        for g in range(GROUP):
            parts.append(picked[g, pl.ds(0, count, stride=2), :].astype(jnp.bfloat16))
            parts.append(picked[g, pl.ds(1, count, stride=2), :].astype(jnp.bfloat16))
            ops.append(w_ref[g])
            ops.append(jnp.zeros((256 - width, width), jnp.bfloat16))
        out_ref[...] += jnp.dot(
            jnp.concatenate(parts, axis=1), jnp.concatenate(ops, axis=0), preferred_element_type=jnp.float32
        )

    slot_copy(0, 0, slots_a).wait()
    pick(rows_a, slots_a)
    apply(rows_b, w_before)
    slot_copy(jnp.minimum(2 * step + 2, groups - 1), 0, slots_a).start()
    slot_copy(0, 1, slots_b).wait()
    pick(rows_b, slots_b)
    apply(rows_a, w_now)
    slot_copy(jnp.minimum(2 * step + 3, groups - 1), 1, slots_b).start()

    @pl.when(step == steps - 1)
    def _():
        slot_copy(0, 0, slots_a).wait()
        slot_copy(0, 1, slots_b).wait()


def far_field(slots, near, top, m2l_ops):
    vectors, count = slots.shape
    pieces, chunk, width = near.shape
    groups = vectors // GROUP
    table_rows = PAD + pieces * chunk + top.shape[0] * top.shape[1]
    return pl.pallas_call(
        far_kernel,
        grid=((groups + 1) // 2,),
        in_specs=[
            pl.BlockSpec(memory_space=pl.ANY),
            pl.BlockSpec(memory_space=pl.ANY),
            pl.BlockSpec(memory_space=pl.ANY),
            pl.BlockSpec((GROUP, width, width), lambda s: (jnp.maximum(2 * s - 1, 0), 0, 0)),
            pl.BlockSpec((GROUP, width, width), lambda s: (2 * s, 0, 0)),
        ],
        out_specs=pl.BlockSpec((count, width), lambda s: (0, 0)),
        out_shape=jax.ShapeDtypeStruct((count, width), jnp.float32),
        scratch_shapes=[
            pltpu.VMEM((2 * table_rows, 128), jnp.float32),
            pltpu.VMEM((GROUP, 2 * count, 128), jnp.float32),
            pltpu.VMEM((GROUP, 2 * count, 128), jnp.float32),
            pltpu.VMEM((2, chunk, width), jnp.bfloat16),
            pltpu.VMEM((2,) + top.shape[1:], jnp.bfloat16),
            pltpu.SMEM((GROUP, count), jnp.int32),
            pltpu.SMEM((GROUP, count), jnp.int32),
            pltpu.SemaphoreType.DMA((2,)),
            pltpu.SemaphoreType.DMA((2,)),
        ],
        compiler_params=pltpu.CompilerParams(vmem_limit_bytes=56 * 2**20),
        name="far_field",
    )(slots.reshape(groups, GROUP, count), near, top, m2l_ops, m2l_ops)


def local(leaf_mult, leaf_list, parent_list, top_list, m2m_ops, m2l_ops, l2l_ops):
    boxes, width = leaf_mult.shape
    vectors = leaf_list.shape[1]
    here = lax.axis_index("morton")
    devices = lax.axis_size("morton")
    parents, tops = boxes // 8, boxes // 64
    chunk = boxes + parents
    parent_mult = ascend(leaf_mult, m2m_ops)
    piece = jnp.concatenate([leaf_mult, parent_mult], axis=0)
    three = jnp.stack([shifted(piece, "morton", RD), piece, shifted(piece, "morton", -RD)])
    groups = [list(range(g, g + RD)) for g in range(0, devices, RD)]
    near = lax.all_gather(three, "morton", axis=0, tiled=True, axis_index_groups=groups)
    top_mult = ascend(parent_mult, m2m_ops)
    padded_top = jnp.pad(top_mult, ((0, TOP_ROWS - tops), (0, 256 - width)))[None]
    all_top = lax.all_gather(padded_top, "morton", axis=0, tiled=True)

    def place(box, per_device):
        device = box // per_device
        return ((device % RD) * 3 + device // RD - here // RD + 1) * chunk + box % per_device

    leaf_row = here * boxes + jnp.arange(boxes, dtype=jnp.int32)[None, :]
    leaf_offset = leaf_list.T
    leaf_slot = jnp.where(leaf_offset != 0, PAD + place(leaf_row + leaf_offset, boxes), 0)
    parent_box = parent_list.T
    parent_slot = jnp.where(parent_box >= 0, PAD + boxes + place(parent_box, parents), 0)
    top_box = top_list.T
    top_slot = jnp.where(top_box >= 0, PAD + 3 * RD * chunk + top_box // tops * TOP_ROWS + top_box % tops, 0)
    spare = -(boxes + parents + tops) % 16
    slots = 2 * jnp.concatenate([leaf_slot, parent_slot, top_slot, jnp.zeros((vectors, spare), jnp.int32)], axis=1)
    far = far_field(slots, near, all_top.reshape(2, -1, 256), m2l_ops)
    leaf_far = far[:boxes]
    parent_far = far[boxes:chunk]
    top_far = far[chunk : chunk + tops]
    top_local = (0.25 * top_far).astype(jnp.bfloat16)
    parent_local = (0.5 * parent_far + descend(top_local, l2l_ops)).astype(jnp.bfloat16)
    return leaf_far + descend(parent_local, l2l_ops)


def solution(mesh):
    return jax.shard_map(
        local,
        mesh=mesh,
        in_specs=(
            P("morton", None),
            P("morton", None),
            P("morton", None),
            P("morton", None),
            P(),
            P(),
            P(),
        ),
        out_specs=P("morton", None),
        check_vma=False,
    )
```

time: 381 us -> 399 us (1.047)
  waiting for transfers between devices: 8.05 us -> 63.6 us
  blocking collectives: 40.2 us -> 0 us
  Pallas kernels: 247 us -> 251 us
    all_gather x0 -> x1, waiting for transfers between devices: none -> 54.9 us  [local(): all_top = lax.all_gather(padded_top, 'morton', axis=0, tiled=True)]
    all_gather x1 -> x0, blocking collectives: 40.2 us -> none  [local(): all_top = lax.all_gather(top_mult, 'morton', axis=0, tiled=True)]
  transfers between devices with their start and end apart: 3 -> 4, of which waited for: 2 -> 4; matrix products, arithmetic and copies ran while one was open for 12% -> 14% of each run, Pallas kernels for 0% -> 0%
where the time goes in v2:
time: 399 us; the launch traced here: 397 us
  Pallas kernels  251 us (63%)
  waiting for transfers between devices  63.6 us (16%)
  local copies, waits for them, and re-layouts  54.7 us (14%)
  between operations  13.6 us (3%)
  other arithmetic  6.18 us (2%)
  starting transfers between devices  5.72 us (1%)
    pallas_call x1, Pallas kernels, far_field(): pl.pallas_call(far_kernel, grid=((groups + 1) // 2,), in_specs=[pl.BlockS...  251 us
    all_gather x1, waiting for transfers between devices, local(): all_top = lax.all_gather(padded_top, 'morton', axis=0, tiled=True)  54.9 us
    unnamed x17, local copies, waits for them, and re-layouts  39.9 us
    all_gather x1, local copies, waits for them, and re-layouts, local(): lax.all_gather(three, 'morton', axis=0, tiled=True, axis_index_groups=gro...  11.5 us
    ppermute x2, waiting for transfers between devices, shifted(): return lax.ppermute(block, axis, route)  8.03 us
  transfers between devices with their start and end apart: 4, of which 4 were waited for; matrix products, arithmetic and copies ran while one was open for 14% of the time, Pallas kernels for 0%

profile of v2, /device:TPU:1, one launch (start us, length us, event | category | flops | bytes accessed | tf_op | source)
XLA Modules:
  0.0 397.4 jit_solution(7868291419502993220)
XLA Ops:
  6.5 1.2 copy.33
  7.7 0.4 reshape.29
  8.1 0.4 convolution_convert_fusion
  8.5 4.4 %collective-permute-start = (bf16[864,152]{0,1:T(8,128)(2,1)S(1)}, bf16[864,152]{0,1:T(8,128)(2,1)S(1)}, u32[]{:S(2)}, u32[]{:S(2)}) collective-permute-start(bf16[864,152]{0,1:T(8,128)(2,1)S(1)} %get-tuple-element.6), channel_id=1, source_target_pairs={{0,8},{1,9},{2,10},{3,11},{4,12},{5,13},{6,14},{7,15},{8,16},{9,17... | collective-permute-start | bytes 787976 | tf_op jit(solution)/shard_map/ppermute | solution.py:17
  12.9 1.3 collective-permute-start.1
  14.2 3.9 collective-permute-done
  18.1 4.2 %collective-permute-done.1 = bf16[864,152]{0,1:T(8,128)(2,1)S(1)} collective-permute-done((bf16[864,152]{0,1:T(8,128)(2,1)S(1)}, bf16[864,152]{0,1:T(8,128)(2,1)S(1)}, u32[]{:S(2)}, u32[]{:S(2)}) %collective-permute-start.1) | collective-permute-done | bytes 262688 | tf_op jit(solution)/shard_map/ppermute | solution.py:17
  22.3 1.1 pad_maximum_fusion
  23.4 0.0 all-gather.6.cloned.1.call-start
  23.4 0.1 copy.34
  23.5 0.1 reshape.31
  23.7 0.2 convolution_convert_fusion.1
  23.8 0.6 pad.4
  24.5 3.3 fusion.7
  27.8 0.3 concatenate.13
  28.1 0.6 copy-done.5
  28.7 0.3 fusion.22
  29.0 0.1 copy.31
  29.3 0.1 copy.32
  29.5 0.1 pad.13.clone
  29.5 37.7 %copy.36.w_before.w_now = bf16[316,152,152]{2,1,0:T(8,128)(2,1)} copy(bf16[316,152,152]{0,2,1:T(8,128)(2,1)} %param.12) | data formatting | bytes 29203456 | tf_op args[5]
  67.3 0.3 copy.40
  67.6 1.3 add_multiply_fusion.slots
  68.9 0.6 all-gather.4.cloned.1.call-done
  69.6 11.5 %copy.35.near = bf16[24,864,152]{2,1,0:T(8,128)(2,1)} copy(bf16[24,864,152]{1,2,0:T(8,128)(2,1)} %all-gather.4.cloned.1.call-done) | data formatting | bytes 12607488 | tf_op jit(solution)/shard_map/all_gather | solution.py:160
  81.1 54.9 %all-gather.6.cloned.1.call-done = bf16[2048,256]{1,0:T(8,128)(2,1)} async-done(((bf16[16,256]{1,0:T(8,128)(2,1)}), bf16[2048,256]{1,0:T(8,128)(2,1)}) %all-gather.6.cloned.1.call-update) | async-done | bytes 1048592 | tf_op jit(solution)/shard_map/all_gather | solution.py:163
  136.0 250.7 %far_field.1 = f32[880,152]{1,0:T(8,128)} custom-call(s32[79,4,880]{2,1,0:T(4,128)} %add_multiply_fusion.slots, bf16[24,864,152]{2,1,0:T(8,128)(2,1)} %copy.35.near, bf16[2,1024,256]{2,1,0:T(8,128)(2,1)} %bitcast.96, bf16[316,152,152]{2,1,0:T(8,128)(2,1)} %copy.36.w_before.w_now, bf16[316,152,152]{2,1,0:T(8,128)(2,1)} %copy.36.w_before.w_now), custom_call_target="tpu_custom_call" | custom-call | tf_op jit(solution)/shard_map/far_field/pallas_call | solution.py:121
  386.7 0.9 fusion.44
  387.6 1.3 fusion.32
  388.9 0.4 copy.41
  389.4 0.1 slice_add_fusion
  389.5 1.0 copy.42
  (22 shorter events, 0.3 us)
Async XLA Ops:
  6.5 1.6 copy-start
  6.5 1.9 copy-start.4
  6.5 63.0 %all-gather.4.cloned.1.call-start = ((), (), s32[]{:S(2)}) async-start(), calls=%async_computation | async-start | bytes 7354368 | tf_op jit(solution)/shard_map/all_gather | solution.py:160
  8.5 9.6 %collective-permute-start = (bf16[864,152]{0,1:T(8,128)(2,1)S(1)}, bf16[864,152]{0,1:T(8,128)(2,1)S(1)}, u32[]{:S(2)}, u32[]{:S(2)}) collective-permute-start(bf16[864,152]{0,1:T(8,128)(2,1)S(1)} %get-tuple-element.6), channel_id=1, source_target_pairs={{0,8},{1,9},{2,10},{3,11},{4,12},{5,13},{6,14},{7,15},{8,16},{9,17... | collective-permute-start | bytes 787976 | tf_op jit(solution)/shard_map/ppermute | solution.py:17
  12.9 9.3 %collective-permute-start.1 = (bf16[864,152]{0,1:T(8,128)(2,1)S(1)}, bf16[864,152]{0,1:T(8,128)(2,1)S(1)}, u32[]{:S(2)}, u32[]{:S(2)}) collective-permute-start(bf16[864,152]{0,1:T(8,128)(2,1)S(1)} %get-tuple-element.6), channel_id=1, source_target_pairs={{8,0},{9,1},{10,2},{11,3},{12,4},{13,5},{14,6},{15,7},{16,8},{17,9... | collective-permute-start | bytes 787976 | tf_op jit(solution)/shard_map/ppermute | solution.py:17
  23.4 112.6 %all-gather.6.cloned.1.call-start = ((), (), s32[]{:S(2)}) async-start(), calls=%async_computation.1 | async-start | bytes 1056768 | tf_op jit(solution)/shard_map/all_gather | solution.py:163
  27.8 0.9 copy-start.5
  27.8 1.4 copy-start.6
  29.5 37.7 %copy-start.3 = (bf16[8,152,152]{2,1,0:T(8,128)(2,1)S(1)}, bf16[8,152,152]{2,1,0:T(8,128)(2,1)}, u32[]{:S(2)}) copy-start(bf16[8,152,152]{2,1,0:T(8,128)(2,1)} %param.13) | copy-start | bytes 1108996
  387.6 1.8 copy-start.2
  389.4 1.1 copy-start.1
Sparse Core Ops, SparseCore 0:
  23.5 45.9 all-gather.3
  72.3 63.6 all-gather.5

commit v3 on v2

--- a/solution.py
+++ b/solution.py
@@ -8,7 +8,6 @@
 RD = 8
 PAD = 8
 GROUP = 4
-TOP_ROWS = 16
 
 
 def shifted(block, axis, distance):
@@ -29,14 +28,18 @@
     return spread.reshape(coarse.shape[0] * 8, coarse.shape[1])
 
 
-def far_kernel(slots, near, top, w_before, w_now, out_ref, table, rows_a, rows_b, stage, top_stage, slots_a, slots_b, sem, stage_sem):
+def far_kernel(slots, near, top, w_0, w_1, w_2, out_ref, table, rows_0, rows_1, rows_2, stage, slots_0, slots_1, slots_2, sem, stage_sem):
     step = pl.program_id(0)
     steps = pl.num_programs(0)
     groups = slots.shape[0]
     count, width = out_ref.shape
 
-    def slot_copy(group, which, buffer):
-        return pltpu.make_async_copy(slots.at[group], buffer, sem.at[which])
+    picked_rows = (rows_0, rows_1, rows_2)
+    slot_buffers = (slots_0, slots_1, slots_2)
+    ops_of = (w_0, w_1, w_2)
+
+    def slot_copy(group, which):
+        return pltpu.make_async_copy(slots.at[group], slot_buffers[which], sem.at[which])
 
     def fill(buffer, base):
         rows, wide = buffer.shape
@@ -51,7 +54,7 @@
             table[pl.ds(start + 1, 16, stride=2), :] = tail
             return carry
 
-        lax.fori_loop(0, rows // 16, sixteen, 0, unroll=2)
+        lax.fori_loop(0, rows // 16, sixteen, 0, unroll=6)
 
     def fill_all(pieces, source, buffers, base):
         def copy(piece, half):
@@ -74,13 +77,14 @@
 
     @pl.when(step == 0)
     def _():
-        slot_copy(0, 0, slots_a).start()
-        slot_copy(1, 1, slots_b).start()
+        slot_copy(0, 0).start()
+        slot_copy(1, 1).start()
         out_ref[...] = jnp.zeros_like(out_ref)
-        rows_b[...] = jnp.zeros_like(rows_b)
+        rows_2[...] = jnp.zeros_like(rows_2)
         table[pl.ds(0, 2 * PAD), :] = jnp.zeros((2 * PAD, 128), jnp.float32)
-        fill_all(near.shape[0], near, stage, PAD)
-        fill_all(top.shape[0], top, top_stage, PAD + near.shape[0] * near.shape[1])
+        pieces, chunk, _ = near.shape
+        fill_all(pieces, near, stage, PAD)
+        fill_all(top.shape[0], top, stage.at[:, pl.ds(0, top.shape[1])], PAD + pieces * chunk)
 
     def pick(into, buffer):
         for g in range(GROUP):
@@ -98,35 +102,38 @@
             jnp.concatenate(parts, axis=1), jnp.concatenate(ops, axis=0), preferred_element_type=jnp.float32
         )
 
-    slot_copy(0, 0, slots_a).wait()
-    pick(rows_a, slots_a)
-    apply(rows_b, w_before)
-    slot_copy(jnp.minimum(2 * step + 2, groups - 1), 0, slots_a).start()
-    slot_copy(0, 1, slots_b).wait()
-    pick(rows_b, slots_b)
-    apply(rows_a, w_now)
-    slot_copy(jnp.minimum(2 * step + 3, groups - 1), 1, slots_b).start()
+    for third in range(3):
+        later = (third + 2) % 3
+        slot_copy(0, third).wait()
+        slot_copy(jnp.minimum(3 * step + third + 2, groups - 1), later).start()
+        pick(picked_rows[third], slot_buffers[third])
+        apply(picked_rows[later], ops_of[third])
 
     @pl.when(step == steps - 1)
     def _():
-        slot_copy(0, 0, slots_a).wait()
-        slot_copy(0, 1, slots_b).wait()
+        slot_copy(0, 0).wait()
+        slot_copy(0, 1).wait()
 
 
 def far_field(slots, near, top, m2l_ops):
     vectors, count = slots.shape
     pieces, chunk, width = near.shape
     groups = vectors // GROUP
+    steps = (groups + 3) // 3
+    last = groups - 1
     table_rows = PAD + pieces * chunk + top.shape[0] * top.shape[1]
+    grouped = jnp.pad(slots.reshape(groups, GROUP, count), ((0, 3 * steps - groups), (0, 0), (0, 0)))
+    block = (GROUP, width, width)
     return pl.pallas_call(
         far_kernel,
-        grid=((groups + 1) // 2,),
+        grid=(steps,),
         in_specs=[
             pl.BlockSpec(memory_space=pl.ANY),
             pl.BlockSpec(memory_space=pl.ANY),
             pl.BlockSpec(memory_space=pl.ANY),
-            pl.BlockSpec((GROUP, width, width), lambda s: (jnp.maximum(2 * s - 1, 0), 0, 0)),
-            pl.BlockSpec((GROUP, width, width), lambda s: (2 * s, 0, 0)),
+            pl.BlockSpec(block, lambda s: (jnp.maximum(3 * s - 1, 0), 0, 0)),
+            pl.BlockSpec(block, lambda s: (jnp.minimum(3 * s, last), 0, 0)),
+            pl.BlockSpec(block, lambda s: (jnp.minimum(3 * s + 1, last), 0, 0)),
         ],
         out_specs=pl.BlockSpec((count, width), lambda s: (0, 0)),
         out_shape=jax.ShapeDtypeStruct((count, width), jnp.float32),
@@ -134,16 +141,17 @@
             pltpu.VMEM((2 * table_rows, 128), jnp.float32),
             pltpu.VMEM((GROUP, 2 * count, 128), jnp.float32),
             pltpu.VMEM((GROUP, 2 * count, 128), jnp.float32),
+            pltpu.VMEM((GROUP, 2 * count, 128), jnp.float32),
             pltpu.VMEM((2, chunk, width), jnp.bfloat16),
-            pltpu.VMEM((2,) + top.shape[1:], jnp.bfloat16),
             pltpu.SMEM((GROUP, count), jnp.int32),
             pltpu.SMEM((GROUP, count), jnp.int32),
-            pltpu.SemaphoreType.DMA((2,)),
+            pltpu.SMEM((GROUP, count), jnp.int32),
+            pltpu.SemaphoreType.DMA((3,)),
             pltpu.SemaphoreType.DMA((2,)),
         ],
         compiler_params=pltpu.CompilerParams(vmem_limit_bytes=56 * 2**20),
         name="far_field",
-    )(slots.reshape(groups, GROUP, count), near, top, m2l_ops, m2l_ops)
+    )(grouped, near, top, m2l_ops, m2l_ops, m2l_ops)
 
 
 def local(leaf_mult, leaf_list, parent_list, top_list, m2m_ops, m2l_ops, l2l_ops):
@@ -159,8 +167,9 @@
     groups = [list(range(g, g + RD)) for g in range(0, devices, RD)]
     near = lax.all_gather(three, "morton", axis=0, tiled=True, axis_index_groups=groups)
     top_mult = ascend(parent_mult, m2m_ops)
-    padded_top = jnp.pad(top_mult, ((0, TOP_ROWS - tops), (0, 256 - width)))[None]
-    all_top = lax.all_gather(padded_top, "morton", axis=0, tiled=True)
+    group_top = lax.all_gather(top_mult, "morton", axis=0, tiled=True, axis_index_groups=groups)
+    strides = [list(range(g, devices, RD)) for g in range(RD)]
+    all_top = lax.all_gather(group_top, "morton", axis=0, tiled=True, axis_index_groups=strides)
 
     def place(box, per_device):
         device = box // per_device
@@ -172,10 +181,10 @@
     parent_box = parent_list.T
     parent_slot = jnp.where(parent_box >= 0, PAD + boxes + place(parent_box, parents), 0)
     top_box = top_list.T
-    top_slot = jnp.where(top_box >= 0, PAD + 3 * RD * chunk + top_box // tops * TOP_ROWS + top_box % tops, 0)
+    top_slot = jnp.where(top_box >= 0, PAD + 3 * RD * chunk + top_box, 0)
     spare = -(boxes + parents + tops) % 16
     slots = 2 * jnp.concatenate([leaf_slot, parent_slot, top_slot, jnp.zeros((vectors, spare), jnp.int32)], axis=1)
-    far = far_field(slots, near, all_top.reshape(2, -1, 256), m2l_ops)
+    far = far_field(slots, near, all_top.reshape(2, -1, width), m2l_ops)
     leaf_far = far[:boxes]
     parent_far = far[boxes:chunk]
     top_far = far[chunk : chunk + tops]

time: 399 us -> 331 us (0.83)
  waiting for transfers between devices: 63.6 us -> 8.07 us
  Pallas kernels: 251 us -> 197 us
  blocking collectives: 0 us -> 37.5 us
    all_gather x1 -> x0, waiting for transfers between devices: 54.9 us -> none  [local(): all_top = lax.all_gather(padded_top, 'morton', axis=0, tiled=True)]
    pallas_call x1, Pallas kernels: 251 us -> 197 us  [far_field(): pl.pallas_call(far_kernel, grid=(steps,), in_specs=[pl.BlockSpec(memory_s...]
    all_gather x0 -> x2, blocking collectives: none -> 37.5 us  [the longest x1 22.9 us: local(): lax.all_gather(group_top, 'morton', axis=0, tiled=True, axis_index_groups...]
    unnamed x17 -> x19, local copies, waits for them, and re-layouts: 39.9 us -> 39.4 us
  transfers between devices with their start and end apart: 4 -> 3, of which waited for: 4 -> 2; matrix products, arithmetic and copies ran while one was open for 14% -> 14% of each run, Pallas kernels for 0% -> 0%
where the time goes in v3:
time: 331 us; the launch traced here: 326 us
  Pallas kernels  197 us (60%)
  local copies, waits for them, and re-layouts  56.1 us (17%)
  blocking collectives  37.5 us (11%)
  between operations  13.6 us (4%)
  waiting for transfers between devices  8.07 us (2%)
  starting transfers between devices  5.68 us (2%)
  other arithmetic  5.17 us (2%)
    pallas_call x1, Pallas kernels, far_field(): pl.pallas_call(far_kernel, grid=(steps,), in_specs=[pl.BlockSpec(memory_s...  197 us
    unnamed x19, local copies, waits for them, and re-layouts  39.4 us
    all_gather x1, blocking collectives, local(): lax.all_gather(group_top, 'morton', axis=0, tiled=True, axis_index_groups...  22.9 us
    all_gather x1, blocking collectives, local(): lax.all_gather(top_mult, 'morton', axis=0, tiled=True, axis_index_groups=...  14.6 us
    all_gather x1, local copies, waits for them, and re-layouts, local(): lax.all_gather(three, 'morton', axis=0, tiled=True, axis_index_groups=gro...  11.6 us
    ppermute x2, waiting for transfers between devices, shifted(): return lax.ppermute(block, axis, route)  8.03 us
  transfers between devices with their start and end apart: 3, of which 2 were waited for; matrix products, arithmetic and copies ran while one was open for 14% of the time, Pallas kernels for 0%

profile of v3, /device:TPU:1, one launch (start us, length us, event | category | flops | bytes accessed | tf_op | source)
XLA Modules:
  0.0 325.8 jit_solution(3471881422207234334)
XLA Ops:
  6.5 1.2 copy.35
  7.7 0.4 reshape.29
  8.1 0.4 convolution_convert_fusion
  8.5 4.4 %collective-permute-start = (bf16[864,152]{0,1:T(8,128)(2,1)S(1)}, bf16[864,152]{0,1:T(8,128)(2,1)S(1)}, u32[]{:S(2)}, u32[]{:S(2)}) collective-permute-start(bf16[864,152]{0,1:T(8,128)(2,1)S(1)} %get-tuple-element.6), channel_id=1, source_target_pairs={{0,8},{1,9},{2,10},{3,11},{4,12},{5,13},{6,14},{7,15},{8,16},{9,17... | collective-permute-start | bytes 787976 | tf_op jit(solution)/shard_map/ppermute | solution.py:16
  12.9 1.3 collective-permute-start.1
  14.2 3.9 %collective-permute-done = bf16[864,152]{0,1:T(8,128)(2,1)S(1)} collective-permute-done((bf16[864,152]{0,1:T(8,128)(2,1)S(1)}, bf16[864,152]{0,1:T(8,128)(2,1)S(1)}, u32[]{:S(2)}, u32[]{:S(2)}) %collective-permute-start) | collective-permute-done | bytes 262688 | tf_op jit(solution)/shard_map/ppermute | solution.py:16
  18.1 4.2 %collective-permute-done.1 = bf16[864,152]{0,1:T(8,128)(2,1)S(1)} collective-permute-done((bf16[864,152]{0,1:T(8,128)(2,1)S(1)}, bf16[864,152]{0,1:T(8,128)(2,1)S(1)}, u32[]{:S(2)}, u32[]{:S(2)}) %collective-permute-start.1) | collective-permute-done | bytes 262688 | tf_op jit(solution)/shard_map/ppermute | solution.py:16
  22.3 1.1 pad_maximum_fusion
  23.4 0.1 copy.36
  23.5 3.3 %fusion.8 = s32[316,768]{1,0:T(8,128)S(1)} fusion(s32[768,316]{0,1:T(8,128)} %param.8, s32[]{:T(128)S(6)} %select_n.60, s32[768]{0:T(1024)S(1)} %iota_add_fusion), kind=kLoop, calls=%fused_computation.18 | loop fusion | flops 9950208 | bytes 1944580 | tf_op jit(solution)/shard_map/jit(_where)/select_n | solution.py:180
  26.8 0.3 concatenate.13
  27.1 0.6 copy-done.5
  27.7 0.3 fusion.23
  28.0 0.1 copy.33
  28.2 0.1 copy.34
  28.5 0.3 add_multiply_fusion
  28.8 1.2 pad.4.slots
  30.0 0.1 reshape.31
  30.2 0.2 fusion
  30.3 14.6 %all-gather = bf16[8,12,152]{2,1,0:T(8,128)(2,1)S(1)} all-gather(bf16[1,12,152]{2,1,0:T(8,128)(2,1)S(1)} %fusion), channel_id=1, replica_groups={{0,1,2,3,4,5,6,7},{8,9,10,11,12,13,14,15},{16,17,18,19,20,21,22,23},{24..., dimensions={0}, use_global_device_ids=true | all-gather | bytes 32832 | tf_op jit(solution)/shard_map/all_gather | solution.py:170
  45.0 0.1 copy.37
  45.1 22.9 %all-gather.1 = bf16[16,96,152]{1,2,0:T(8,128)(2,1)S(1)} all-gather(bf16[1,96,152]{1,2,0:T(8,128)(2,1)S(1)} %copy.37), channel_id=1, replica_groups={{0,8,16,24,32,40,48,56,64,72,80,88,96,104,112,120},{1,9,17,25,33,41,49,..., dimensions={0}, use_global_device_ids=true | all-gather | bytes 496128 | tf_op jit(solution)/shard_map/all_gather | solution.py:172
  68.0 1.3 copy.38
  69.3 37.1 %copy.40.w_0.w_1.w_2 = bf16[316,152,152]{2,1,0:T(8,128)(2,1)} copy(bf16[316,152,152]{0,2,1:T(8,128)(2,1)} %param.12) | data formatting | bytes 29203456 | tf_op args[5]
  106.4 0.3 copy.45
  106.7 11.6 %copy.39.near = bf16[24,864,152]{2,1,0:T(8,128)(2,1)} copy(bf16[24,864,152]{1,2,0:T(8,128)(2,1)} %all-gather.4.cloned.1.call-done) | data formatting | bytes 12607488 | tf_op jit(solution)/shard_map/all_gather | solution.py:168
  118.3 196.8 %far_field.1 = f32[880,152]{1,0:T(8,128)} custom-call(s32[81,4,880]{2,1,0:T(4,128)} %pad.4.slots, bf16[24,864,152]{2,1,0:T(8,128)(2,1)} %copy.39.near, bf16[2,768,152]{2,1,0:T(8,128)(2,1)} %bitcast.78, bf16[316,152,152]{2,1,0:T(8,128)(2,1)} %copy.40.w_0.w_1.w_2, bf16[316,152,152]{2,1,0:T(8,128)(2,1)} %copy.40.w_0.w_1.w_2, ...), custom_call_target="tpu_custom_call" | custom-call | tf_op jit(solution)/shard_map/far_field/pallas_call | solution.py:127
  315.1 0.9 fusion.38
  316.0 1.3 fusion.33
  317.4 0.4 copy.46
  317.8 0.1 slice_add_fusion
  317.9 1.0 copy.47
  (24 shorter events, 0.3 us)
Async XLA Ops:
  6.5 1.6 copy-start
  6.5 1.9 copy-start.4
  6.5 100.2 %all-gather.4.cloned.1.call-start = ((), (), s32[]{:S(2)}) async-start(), calls=%async_computation | async-start | bytes 7354368 | tf_op jit(solution)/shard_map/all_gather | solution.py:168
  8.5 9.6 %collective-permute-start = (bf16[864,152]{0,1:T(8,128)(2,1)S(1)}, bf16[864,152]{0,1:T(8,128)(2,1)S(1)}, u32[]{:S(2)}, u32[]{:S(2)}) collective-permute-start(bf16[864,152]{0,1:T(8,128)(2,1)S(1)} %get-tuple-element.6), channel_id=1, source_target_pairs={{0,8},{1,9},{2,10},{3,11},{4,12},{5,13},{6,14},{7,15},{8,16},{9,17... | collective-permute-start | bytes 787976 | tf_op jit(solution)/shard_map/ppermute | solution.py:16
  12.9 9.3 %collective-permute-start.1 = (bf16[864,152]{0,1:T(8,128)(2,1)S(1)}, bf16[864,152]{0,1:T(8,128)(2,1)S(1)}, u32[]{:S(2)}, u32[]{:S(2)}) collective-permute-start(bf16[864,152]{0,1:T(8,128)(2,1)S(1)} %get-tuple-element.6), channel_id=1, source_target_pairs={{8,0},{9,1},{10,2},{11,3},{12,4},{13,5},{14,6},{15,7},{16,8},{17,9... | collective-permute-start | bytes 787976 | tf_op jit(solution)/shard_map/ppermute | solution.py:16
  26.8 0.9 copy-start.5
  26.8 1.4 copy-start.6
  69.3 37.1 %copy-start.3 = (bf16[8,152,152]{2,1,0:T(8,128)(2,1)S(1)}, bf16[8,152,152]{2,1,0:T(8,128)(2,1)}, u32[]{:S(2)}) copy-start(bf16[8,152,152]{2,1,0:T(8,128)(2,1)} %param.13) | copy-start | bytes 1108996
  316.0 1.8 copy-start.2
  317.8 1.1 copy-start.1
Sparse Core Ops, SparseCore 0:
  23.5 46.1 all-gather.3

commit v4 on v3

--- a/solution.py
+++ b/solution.py
@@ -166,7 +166,7 @@
     three = jnp.stack([shifted(piece, "morton", RD), piece, shifted(piece, "morton", -RD)])
     groups = [list(range(g, g + RD)) for g in range(0, devices, RD)]
     near = lax.all_gather(three, "morton", axis=0, tiled=True, axis_index_groups=groups)
-    top_mult = ascend(parent_mult, m2m_ops)
+    near, top_mult = lax.optimization_barrier((near, ascend(parent_mult, m2m_ops)))
     group_top = lax.all_gather(top_mult, "morton", axis=0, tiled=True, axis_index_groups=groups)
     strides = [list(range(g, devices, RD)) for g in range(RD)]
     all_top = lax.all_gather(group_top, "morton", axis=0, tiled=True, axis_index_groups=strides)

time: 331 us -> 331 us (level)
    all_gather x1 -> x0, local copies, waits for them, and re-layouts: 11.6 us -> none  [local(): lax.all_gather(three, 'morton', axis=0, tiled=True, axis_index_groups=gro...]
    optimization_barrier x0 -> x1, local copies, waits for them, and re-layouts: none -> 11.6 us  [local(): lax.optimization_barrier((near, ascend(parent_mult, m2m_ops)))]
  transfers between devices with their start and end apart: 3 -> 3, of which waited for: 2 -> 3; matrix products, arithmetic and copies ran while one was open for 14% -> 14% of each run, Pallas kernels for 0% -> 0%
where the time goes in v4:
time: 331 us; the launch traced here: 326 us
  Pallas kernels  197 us (60%)
  local copies, waits for them, and re-layouts  57 us (17%)
  blocking collectives  35.5 us (11%)
  between operations  13.6 us (4%)
  waiting for transfers between devices  8.97 us (3%)
  starting transfers between devices  5.68 us (2%)
  other arithmetic  5.17 us (2%)
    pallas_call x1, Pallas kernels, far_field(): pl.pallas_call(far_kernel, grid=(steps,), in_specs=[pl.BlockSpec(memory_s...  197 us
    unnamed x19, local copies, waits for them, and re-layouts  40.3 us
    all_gather x1, blocking collectives, local(): lax.all_gather(group_top, 'morton', axis=0, tiled=True, axis_index_groups...  22 us
    all_gather x1, blocking collectives, local(): lax.all_gather(top_mult, 'morton', axis=0, tiled=True, axis_index_groups=...  13.6 us
    optimization_barrier x1, local copies, waits for them, and re-layouts, local(): lax.optimization_barrier((near, ascend(parent_mult, m2m_ops)))  11.6 us
    ppermute x2, waiting for transfers between devices, shifted(): return lax.ppermute(block, axis, route)  8.03 us
  transfers between devices with their start and end apart: 3, of which 3 were waited for; matrix products, arithmetic and copies ran while one was open for 14% of the time, Pallas kernels for 0%

profile of v4, /device:TPU:1, one launch (start us, length us, event | category | flops | bytes accessed | tf_op | source)
XLA Modules:
  0.0 325.5 jit_solution(4553282611569494142)
XLA Ops:
  6.5 1.2 copy.35
  7.7 0.4 reshape.29
  8.1 0.4 convolution_convert_fusion
  8.5 4.4 %collective-permute-start = (bf16[864,152]{0,1:T(8,128)(2,1)S(1)}, bf16[864,152]{0,1:T(8,128)(2,1)S(1)}, u32[]{:S(2)}, u32[]{:S(2)}) collective-permute-start(bf16[864,152]{0,1:T(8,128)(2,1)S(1)} %get-tuple-element.10), channel_id=1, source_target_pairs={{0,8},{1,9},{2,10},{3,11},{4,12},{5,13},{6,14},{7,15},{8,16},{9,17... | collective-permute-start | bytes 787976 | tf_op jit(solution)/shard_map/ppermute | solution.py:16
  12.9 1.3 collective-permute-start.1
  14.2 3.9 %collective-permute-done = bf16[864,152]{0,1:T(8,128)(2,1)S(1)} collective-permute-done((bf16[864,152]{0,1:T(8,128)(2,1)S(1)}, bf16[864,152]{0,1:T(8,128)(2,1)S(1)}, u32[]{:S(2)}, u32[]{:S(2)}) %collective-permute-start) | collective-permute-done | bytes 262688 | tf_op jit(solution)/shard_map/ppermute | solution.py:16
  18.1 4.2 %collective-permute-done.1 = bf16[864,152]{0,1:T(8,128)(2,1)S(1)} collective-permute-done((bf16[864,152]{0,1:T(8,128)(2,1)S(1)}, bf16[864,152]{0,1:T(8,128)(2,1)S(1)}, u32[]{:S(2)}, u32[]{:S(2)}) %collective-permute-start.1) | collective-permute-done | bytes 262688 | tf_op jit(solution)/shard_map/ppermute | solution.py:16
  22.3 1.1 pad_maximum_fusion
  23.5 3.3 %fusion.7 = s32[316,768]{1,0:T(8,128)S(1)} fusion(s32[768,316]{0,1:T(8,128)} %param.8, s32[]{:T(128)S(6)} %select_n.60, s32[768]{0:T(1024)S(1)} %iota_add_fusion), kind=kLoop, calls=%fused_computation.17 | loop fusion | flops 9950208 | bytes 1944580 | tf_op jit(solution)/shard_map/jit(_where)/select_n | solution.py:180
  26.8 0.3 concatenate.13
  27.1 0.6 copy-done.5
  27.7 0.3 fusion.22
  28.0 0.1 copy.33
  28.2 0.1 copy.34
  28.5 0.3 add_multiply_fusion
  28.8 1.2 pad.4.slots
  30.0 0.1 reshape.31
  30.2 38.0 %copy.40.w_0.w_1.w_2 = bf16[316,152,152]{2,1,0:T(8,128)(2,1)} copy(bf16[316,152,152]{0,2,1:T(8,128)(2,1)} %param.12) | data formatting | bytes 29203456 | tf_op args[5]
  68.1 0.3 copy.45
  68.5 0.2 convolution_convert_fusion.1
  68.7 0.9 all-gather.4.cloned.1.call-done
  69.6 11.6 %copy.39.near = bf16[24,864,152]{2,1,0:T(8,128)(2,1)} copy(bf16[24,864,152]{1,2,0:T(8,128)(2,1)} %all-gather.4.cloned.1.call-done) | data formatting | bytes 12607488 | tf_op jit(solution)/shard_map/optimization_barrier | solution.py:169
  81.1 13.6 %all-gather = bf16[8,12,152]{2,1,0:T(8,128)(2,1)S(1)} all-gather(bf16[1,12,152]{2,1,0:T(8,128)(2,1)S(1)} %bitcast.82), channel_id=1, replica_groups={{0,1,2,3,4,5,6,7},{8,9,10,11,12,13,14,15},{16,17,18,19,20,21,22,23},{24..., dimensions={0}, use_global_device_ids=true | all-gather | bytes 32832 | tf_op jit(solution)/shard_map/all_gather | solution.py:170
  94.7 0.1 copy.37
  94.8 22.0 %all-gather.1 = bf16[16,96,152]{1,2,0:T(8,128)(2,1)S(1)} all-gather(bf16[1,96,152]{1,2,0:T(8,128)(2,1)S(1)} %copy.37), channel_id=1, replica_groups={{0,8,16,24,32,40,48,56,64,72,80,88,96,104,112,120},{1,9,17,25,33,41,49,..., dimensions={0}, use_global_device_ids=true | all-gather | bytes 496128 | tf_op jit(solution)/shard_map/all_gather | solution.py:172
  116.8 1.2 copy.38
  118.0 196.8 %far_field.1 = f32[880,152]{1,0:T(8,128)} custom-call(s32[81,4,880]{2,1,0:T(4,128)} %pad.4.slots, bf16[24,864,152]{2,1,0:T(8,128)(2,1)} %copy.39.near, bf16[2,768,152]{2,1,0:T(8,128)(2,1)} %bitcast.77, bf16[316,152,152]{2,1,0:T(8,128)(2,1)} %copy.40.w_0.w_1.w_2, bf16[316,152,152]{2,1,0:T(8,128)(2,1)} %copy.40.w_0.w_1.w_2, ...), custom_call_target="tpu_custom_call" | custom-call | tf_op jit(solution)/shard_map/far_field/pallas_call | solution.py:127
  314.8 0.9 fusion.37
  315.7 1.3 fusion.32
  317.1 0.4 copy.46
  317.5 0.1 slice_add_fusion
  317.6 1.0 copy.47
  (24 shorter events, 0.4 us)
Async XLA Ops:
  6.5 1.6 copy-start
  6.5 1.9 copy-start.4
  6.5 63.0 %all-gather.4.cloned.1.call-start = ((), (), s32[]{:S(2)}) async-start(), calls=%async_computation | async-start | bytes 7354368 | tf_op jit(solution)/shard_map/all_gather | solution.py:168
  8.5 9.6 %collective-permute-start = (bf16[864,152]{0,1:T(8,128)(2,1)S(1)}, bf16[864,152]{0,1:T(8,128)(2,1)S(1)}, u32[]{:S(2)}, u32[]{:S(2)}) collective-permute-start(bf16[864,152]{0,1:T(8,128)(2,1)S(1)} %get-tuple-element.10), channel_id=1, source_target_pairs={{0,8},{1,9},{2,10},{3,11},{4,12},{5,13},{6,14},{7,15},{8,16},{9,17... | collective-permute-start | bytes 787976 | tf_op jit(solution)/shard_map/ppermute | solution.py:16
  12.9 9.3 %collective-permute-start.1 = (bf16[864,152]{0,1:T(8,128)(2,1)S(1)}, bf16[864,152]{0,1:T(8,128)(2,1)S(1)}, u32[]{:S(2)}, u32[]{:S(2)}) collective-permute-start(bf16[864,152]{0,1:T(8,128)(2,1)S(1)} %get-tuple-element.10), channel_id=1, source_target_pairs={{8,0},{9,1},{10,2},{11,3},{12,4},{13,5},{14,6},{15,7},{16,8},{17,9... | collective-permute-start | bytes 787976 | tf_op jit(solution)/shard_map/ppermute | solution.py:16
  26.8 0.9 copy-start.5
  26.8 1.4 copy-start.6
  30.2 38.0 %copy-start.3 = (bf16[8,152,152]{2,1,0:T(8,128)(2,1)S(1)}, bf16[8,152,152]{2,1,0:T(8,128)(2,1)}, u32[]{:S(2)}) copy-start(bf16[8,152,152]{2,1,0:T(8,128)(2,1)} %param.13) | copy-start | bytes 1108996
  315.7 1.8 copy-start.2
  317.5 1.1 copy-start.1
Sparse Core Ops, SparseCore 0:
  23.5 45.9 all-gather.3
